TPU v7x, 32 devices: a whole 2x2x4 slice. The times are simulated.
32 devices in a mesh: groups: 2 (over y), filt: 4 (over z), sp: 2 (over x), in: 2 (over core).
Axes of the slice: x: 2, y: 2, z: 4, core: 2. Of those that a mesh axis runs over, the one named last changes fastest.
Arguments:
- image: bfloat16 [16, 256, 1024], P(('groups', 'sp', 'filt'), None, 'in'), parts along dimension 0, may hold values from -6 to 6
- weight: bfloat16 [3, 3, 1024, 1024], P(None, None, 'filt'), may hold values from -0.0625 to 0.0625
- bias: float32 [1024], P('filt'), may hold values from -3 to 3
- cotangent: bfloat16 [16, 1024, 256], P(('groups', 'sp'), 'filt'), parts along dimension 0, may hold values from -0.029907227 to 0.029907227
Outputs:
- output: bfloat16 [16, 1024, 256], P(('groups', 'sp', 'filt'), None, 'in'), parts along dimension 0
- grad_weight: float32 [6, 3, 1024, 1024], P('groups', None, 'filt', 'in'), parts along dimension 0
- grad_bias: float32 [2048], P(('groups', 'filt')), parts along dimension 0
There are 2 independent parts, one for each index of `groups`. A program takes and returns all parts, laid end to end along the dimension named above; an argument that names none is the same for every part. Nothing has to cross between parts.
All inputs are finite; a program needn't handle non-finite values.
Results may differ from a plain program's by a relative error of at most 0.0055.
Values may be sent and summed in bfloat16 or wider, within the bound.
No kernel may reach another device: no remote copies, remote signals or barrier semaphores. Data moves between devices by JAX's collectives and lax.ppermute only.
A program may use at most 64 MiB of HBM per device.

v0:
```python
import functools
import math

import jax
import jax.numpy as jnp
from jax import lax
from jax.experimental import pallas as pl
from jax.experimental.pallas import tpu as pltpu
from jax.sharding import PartitionSpec as P

MIB = 1024 * 1024


def params(*arrays):
    held = sum(math.prod(shape) * size for shape, size in arrays)
    return pltpu.CompilerParams(vmem_limit_bytes=max(20 * MIB, held * 5 // 4 + 8 * MIB))


def shifted_ring(axis, shift):
    size = lax.axis_size(axis)
    return [(i, (i + shift) % size) for i in range(size)]


def folded_ring(axis, shift):
    size = lax.axis_size(axis)
    order = [0, *range(1, size, 2), *reversed(range(2, size, 2))]
    return [(order[i], order[(i + shift) % size]) for i in range(size)]


def folded_behind(axis, size, by):
    index = lax.axis_index(axis)
    back = size - lax.div(index, 2)
    place = jnp.where(lax.rem(index, 2) == 1, lax.div(index + 1, 2), lax.rem(back, size))
    place = lax.rem(place + (size - by), size)
    out = 2 * place - 1
    return jnp.where(place == 0, 0, jnp.where(place <= size // 2, out, 2 * (size - place)))


def gather_blocks(image):
    n_filt, n_sp = lax.axis_size("filt"), lax.axis_size("sp")
    onward, outward = shifted_ring("sp", 1), folded_ring("filt", 1)
    blocks = [[None] * n_filt for _ in range(n_sp)]
    blocks[0][0] = image
    last = n_filt - 1
    for k in range(n_filt):
        if k:
            blocks[0][k] = lax.ppermute(blocks[0][k - 1], "filt", outward)
        for j in range(1, n_sp):
            if k < max(last, 1):
                blocks[j][k] = lax.ppermute(blocks[j - 1][k], "sp", onward)
    return blocks


def send_held(blocks, cotangent, after):
    n_filt, n_sp = len(blocks[0]), len(blocks)
    first = [side[0] for side in blocks[1:]]
    half, *first = hold(cotangent, first, after)
    halves = [half]
    for j in range(1, n_sp):
        if n_filt > 1:
            blocks[j][-1] = lax.ppermute(first[j - 1], "filt", folded_ring("filt", -1))
        halves.append(lax.ppermute(halves[-1], "sp", shifted_ring("sp", 1)))
    return halves


def move_columns(values, by):
    size = values.shape[1]
    column = lax.broadcasted_iota(jnp.int32, values.shape, 1)
    edge = 0 if by == 1 else size - 1
    return jnp.where(column == edge, jnp.zeros_like(values), pltpu.roll(values, by % size, 1))


VMEM = pl.BlockSpec(memory_space=pltpu.VMEM)
ANY = pl.BlockSpec(memory_space=pl.ANY)


def behind(axis, size, by):
    return lax.rem(lax.axis_index(axis) + (size - by), size)


def hold_kernel(n_blocks, n_after, cotangent, *refs):
    blocks, (half, *copies, sems) = refs[:n_blocks], refs[n_blocks + n_after :]
    rows = half.shape[0]
    moves = [(cotangent.at[pl.ds(lax.axis_index("in") * rows, rows)], half)]
    moves += zip(blocks, copies)
    moves = [pltpu.make_async_copy(*move, sems.at[i]) for i, move in enumerate(moves)]
    for move in moves:
        move.start()
    for move in moves:
        move.wait()


def hold(cotangent, blocks, after):
    shape = (cotangent.shape[0] // 2,) + cotangent.shape[1:]
    held = [jax.ShapeDtypeStruct(block.shape, block.dtype) for block in blocks]
    return pl.pallas_call(
        functools.partial(hold_kernel, len(blocks), len(after)),
        out_shape=[jax.ShapeDtypeStruct(shape, cotangent.dtype), *held],
        in_specs=[ANY] * (1 + len(blocks) + len(after)),
        out_specs=[VMEM] * (1 + len(blocks)),
        scratch_shapes=[pltpu.SemaphoreType.DMA((1 + len(blocks),))],
        compiler_params=params((shape, 2), *((block.shape, 2) for block in blocks)),
        cost_estimate=pl.CostEstimate(
            flops=0, bytes_accessed=4 * math.prod(shape), transcendentals=0
        ),
    )(cotangent, *blocks, *after)


def arrange_kernel(weight, bias, *refs):
    taps, bias_col, sems = refs[-3:]
    depth = taps.shape[1] // 3
    own = weight.shape[2]
    half = lax.axis_index("in")
    copies = [
        pltpu.make_async_copy(
            weight.at[a, b, :, pl.ds(pl.multiple_of(half * depth, depth), depth)],
            taps.at[pl.ds(a * own, own), pl.ds(b * depth, depth)],
            sems.at[a * 3 + b],
        )
        for a in range(3)
        for b in range(3)
    ]
    for copy in copies:
        copy.start()
    bias_col[...] = jnp.broadcast_to(bias[...], (128, own)).T[:, :1]
    for copy in copies:
        copy.wait()


def arrange(weight, bias, depth, after):
    own = weight.shape[2]
    shape = (3 * own, 3 * depth)
    return pl.pallas_call(
        arrange_kernel,
        out_shape=(
            jax.ShapeDtypeStruct(shape, weight.dtype),
            jax.ShapeDtypeStruct((own, 1), bias.dtype),
        ),
        in_specs=[ANY, VMEM] + [ANY] * len(after),
        out_specs=(VMEM, VMEM),
        scratch_shapes=[pltpu.SemaphoreType.DMA((9,))],
        compiler_params=params((shape, 2)),
        cost_estimate=pl.CostEstimate(
            flops=0, bytes_accessed=36 * own * depth, transcendentals=0
        ),
    )(weight, bias.reshape(1, own), *after)


def block_place(index, n_filt, n_sp):
    j, k = divmod(index, n_filt)
    return behind("sp", n_sp, j) * n_filt + folded_behind("filt", n_filt, k)


def turn_row(turned, row):
    values = row.T
    depth = values.shape[0]
    turned[pl.ds(0, depth), :] = move_columns(values, 1)
    turned[pl.ds(depth, depth), :] = values
    turned[pl.ds(2 * depth, depth), :] = move_columns(values, -1)


def add_row(total, slot, taps, row, turned):
    own = taps.shape[0] // 3
    turn_row(turned, row)
    product = jnp.dot(taps[...], turned[...], preferred_element_type=jnp.float32)
    for a in range(3):
        total[slot + 1 - a] += product[a * own : (a + 1) * own]


def add_blocks_kernel(where, n_filt, n_sp, fresh, taps, *refs):
    *blocks, total, turned = refs if fresh else refs[1:]
    rows_dev = blocks[0].shape[0]
    total[...] = jnp.zeros(total.shape, total.dtype) if fresh else refs[0][...]
    for index, (block, (j, k)) in enumerate(zip(blocks, where)):
        place = block_place(j * n_filt + k, n_filt, n_sp)
        for i in range(rows_dev):
            at = index * rows_dev + i
            add_row(total, place * rows_dev + i + 1, taps, block[i], turned.at[at])


def add_blocks(taps, sides, where, side_rows, begun=()):
    n_sp, n_filt = len(sides), len(sides[0])
    blocks = [sides[j][k] for j, k in where]
    rows_dev, width, depth = blocks[0].shape
    own = taps.shape[0] // 3
    shape = (n_sp * side_rows + 2, own, width)
    turned = (len(blocks) * rows_dev, 3 * depth, width)
    return pl.pallas_call(
        functools.partial(add_blocks_kernel, where, n_filt, n_sp, not begun),
        out_shape=jax.ShapeDtypeStruct(shape, jnp.float32),
        in_specs=[VMEM] * (1 + len(begun) + len(blocks)),
        out_specs=VMEM,
        scratch_shapes=[pltpu.VMEM(turned, blocks[0].dtype)],
        compiler_params=params((turned, 2), (shape, 8), (taps.shape, 4)),
        cost_estimate=pl.CostEstimate(
            flops=(1 if begun else 30) * len(blocks) * rows_dev * own * width * depth,
            bytes_accessed=1,
            transcendentals=0,
        ),
    )(taps, *begun, *blocks)


def last_rows_kernel(n_filt, n_sp, j, n_after, taps, begun, *refs):
    *blocks, out, total, turned = refs[n_after:]
    rows_dev = blocks[0].shape[0]
    side_rows, own = total.shape[0] - 2, total.shape[1]
    side = behind("sp", n_sp, j)
    total[...] = begun[pl.ds(side * side_rows, side_rows + 2)]

    def slot_of(other):
        place = block_place(other * n_filt + n_filt - 1, n_filt, n_sp)
        return place * rows_dev - side * side_rows + 1

    for other, block in enumerate(blocks, 1):
        for i in range(rows_dev):
            if other == j:
                add_row(total, slot_of(other) + i, taps, block[i], turned.at[i])
        if other != j:
            for i, at, edge, a in ((rows_dev - 1, 0, 1, 0), (0, side_rows + 1, side_rows, 2)):

                @pl.when(slot_of(other) + i == at)
                def _():
                    turn_row(turned.at[0], block[i])
                    rows = taps[pl.ds(a * own, own), :]
                    product = jnp.dot(rows, turned[0], preferred_element_type=jnp.float32)
                    total[edge] += product

    out[...] = total[pl.ds(1, side_rows)]


def last_rows(taps, begun, sides, j, side_rows, after=()):
    n_sp, n_filt = len(sides), len(sides[0])
    blocks = [side[-1] for side in sides[1:]]
    rows_dev, width, depth = blocks[0].shape
    own = taps.shape[0] // 3
    out = (side_rows, own, width)
    total = (side_rows + 2, own, width)
    turned = (rows_dev, 3 * depth, width)
    return pl.pallas_call(
        functools.partial(last_rows_kernel, n_filt, n_sp, j, len(after)),
        out_shape=jax.ShapeDtypeStruct(out, jnp.float32),
        in_specs=[VMEM] * 2 + [ANY] * len(after) + [VMEM] * len(blocks),
        out_specs=VMEM,
        scratch_shapes=[
            pltpu.VMEM(total, jnp.float32),
            pltpu.VMEM(turned, blocks[0].dtype),
        ],
        compiler_params=params(
            (turned, 2 + n_sp), (total, 12), (begun.shape, 4), (taps.shape, 4)
        ),
        cost_estimate=pl.CostEstimate(
            flops=18 * rows_dev * own * width * depth,
            bytes_accessed=18 * own * depth,
            transcendentals=0,
        ),
    )(taps, begun, *after, *blocks)


def silu_parts(shifted, cotangent):
    sigmoid_v = 0.5 * jnp.tanh(0.5 * shifted) + 0.5
    slope = sigmoid_v * (1.0 + shifted * (1.0 - sigmoid_v))
    grad_out = (cotangent.astype(jnp.float32) * slope).astype(jnp.bfloat16)
    return sigmoid_v, grad_out


def silu_kernel(n_filt, mine, theirs, bias, cotangent, grad_out, *activated):
    rows, _, half = activated[0].shape

    for k in range(n_filt):
        first = behind("filt", n_filt, n_filt - k if k else 0) * rows

        @pl.loop(0, rows)
        def _(i):
            r = first + i
            shifted = (mine[r] + theirs[r]) + bias[...]
            sigmoid_v, grad_out[r] = silu_parts(shifted, cotangent[r])
            value = (shifted * sigmoid_v).astype(activated[k].dtype)
            activated[k][i] = jnp.where(
                lax.axis_index("in") == 0, value[:, :half], value[:, half:]
            )


def silu(mine, theirs, bias, cotangent, n_filt):
    rows, own, width = cotangent.shape
    return pl.pallas_call(
        functools.partial(silu_kernel, n_filt),
        out_shape=[jax.ShapeDtypeStruct((rows, own, width), jnp.bfloat16)]
        + [jax.ShapeDtypeStruct((rows // n_filt, own, width // 2), jnp.bfloat16)] * n_filt,
        in_specs=[VMEM] * 4,
        out_specs=[VMEM] * (1 + n_filt),
        compiler_params=params((cotangent.shape, 16)),
        cost_estimate=pl.CostEstimate(
            flops=10 * rows * own * width,
            bytes_accessed=13 * rows * own * width,
            transcendentals=rows * own * width,
        ),
    )(mine, theirs, bias, cotangent)


def shift_grads(grads, grad_out, row):
    own, width = grad_out.shape
    at = pl.ds(pl.multiple_of(row * width, width), width)
    grads[pl.ds(0, own), at] = move_columns(grad_out, -1)
    grads[pl.ds(own, own), at] = grad_out
    grads[pl.ds(2 * own, own), at] = move_columns(grad_out, 1)


def panel_copies(panel, blocks, n_filt, n_sp, sems):
    rows_dev, width, _ = blocks[0].shape
    copies = []
    for index, block in enumerate(blocks):
        place = block_place(index, n_filt, n_sp)
        for i in range(rows_dev):
            at = pl.multiple_of((place * rows_dev + i + 1) * width, width)
            to = panel.at[pl.ds(at, width), :]
            copies.append(pltpu.make_async_copy(block.at[i], to, sems.at[index * rows_dev + i]))
    return copies


def gradient_kernel(n_filt, n_sp, bias, own_grad, *refs):
    others, refs = refs[: 4 * (n_sp - 1)], refs[4 * (n_sp - 1) :]
    *blocks, weight_sum, bias_sum, formed = refs[: n_sp * n_filt + 3]
    grads, (panel, stage, sems, row_sems) = refs[-4 - n_sp : -4], refs[-4:]
    side_rows, own, width = own_grad.shape
    half_rows = side_rows // 2
    half = lax.axis_index("in")
    copies = panel_copies(panel, blocks, n_filt, n_sp, row_sems)
    for copy in copies:
        copy.start()
    zeros = jnp.zeros((width, panel.shape[1]), panel.dtype)
    panel[pl.ds(0, width), :] = zeros
    panel[pl.ds((n_sp * side_rows + 1) * width, width), :] = zeros
    for r in range(side_rows):
        shift_grads(grads[0], own_grad[r], r)
    for copy in copies:
        copy.wait()

    def tap_gradient(j, a):
        first = (behind("sp", n_sp, j) * side_rows + a) * width
        window = panel[pl.ds(pl.multiple_of(first, width), side_rows * width), :]
        return jnp.dot(grads[j][...], window, preferred_element_type=jnp.float32)

    def copy_out(a, b):
        return pltpu.make_async_copy(stage.at[a, b], weight_sum.at[a, b], sems.at[a, b])

    for a in range(3):
        stage[a] = tap_gradient(0, a).reshape(stage.shape[1:])
    for j in range(1, n_sp):
        mine, theirs, near, far = others[4 * (j - 1) : 4 * j]
        for h, cotangent in enumerate((near, far)):
            start = (half if h == 0 else 1 - half) * half_rows
            for r in range(half_rows):
                shifted = (mine[start + r] + theirs[start + r]) + bias[...]
                _, grad_out = silu_parts(shifted, cotangent[r])
                shift_grads(grads[j], grad_out, start + r)

    for a in range(3):
        for j in range(1, n_sp):
            product = tap_gradient(j, a)
            for b in range(3):
                stage[a, b] += product[b * own : (b + 1) * own]
                if j == n_sp - 1:
                    copy_out(a, b).start()

    total = jnp.zeros((16, own), jnp.float32)
    for side in grads:
        total += lax.dot_general(
            jnp.ones((16, side.shape[1]), side.dtype),
            side[pl.ds(own, own), :],
            (((1,), (1,)), ((), ())),
            preferred_element_type=jnp.float32,
        )
    bias_sum[...] = total[:1]
    formed[...] = jnp.zeros(formed.shape, formed.dtype)
    for a in range(3):
        for b in range(3):
            copy_out(a, b).wait()


def gradient(bias, own_grad, others, sides):
    n_sp, n_filt = len(sides), len(sides[0])
    blocks = [block for side in sides for block in side]
    side_rows, own, width = own_grad.shape
    depth = blocks[0].shape[2]
    all_rows = n_sp * side_rows
    panel = ((all_rows + 2) * width, depth)
    grads = (3 * own, side_rows * width)
    total = (3, 3, own, depth)
    return pl.pallas_call(
        functools.partial(gradient_kernel, n_filt, n_sp),
        out_shape=[
            jax.ShapeDtypeStruct(total, jnp.float32),
            jax.ShapeDtypeStruct((1, own), jnp.float32),
            jax.ShapeDtypeStruct((8, 128), jnp.float32),
        ],
        in_specs=[VMEM] * (2 + len(others)) + [ANY] * len(blocks),
        out_specs=[ANY, VMEM, VMEM],
        scratch_shapes=[
            *[pltpu.VMEM(grads, jnp.bfloat16)] * n_sp,
            pltpu.VMEM(panel, blocks[0].dtype),
            pltpu.VMEM(total, jnp.float32),
            pltpu.SemaphoreType.DMA((3, 3)),
            pltpu.SemaphoreType.DMA((all_rows,)),
        ],
        compiler_params=params(
            (grads, 2 * n_sp), (panel, 2), (total, 6), ((all_rows, own, width), 12)
        ),
        cost_estimate=pl.CostEstimate(
            flops=18 * all_rows * own * width * depth,
            bytes_accessed=36 * own * depth + 2 * all_rows * width * depth,
            transcendentals=all_rows * own * width,
        ),
    )(bias, own_grad, *others, *blocks)


def place_kernel(*refs):
    *pieces, _, output, sems = refs
    own = pieces[0].shape[1]
    copies = []
    for k, piece in enumerate(pieces):
        at = pl.multiple_of(behind("filt", len(pieces), k) * own, own)
        rows = output.at[:, pl.ds(at, own), :]
        copies.append(pltpu.make_async_copy(piece, rows, sems.at[k]))
    for copy in copies:
        copy.start()
    for copy in copies:
        copy.wait()


def place_pieces(pieces, after):
    rows, own, half = pieces[0].shape
    return pl.pallas_call(
        place_kernel,
        out_shape=jax.ShapeDtypeStruct((rows, len(pieces) * own, half), pieces[0].dtype),
        in_specs=[VMEM] * (len(pieces) + 1),
        out_specs=ANY,
        scratch_shapes=[pltpu.SemaphoreType.DMA((len(pieces),))],
        compiler_params=params((pieces[0].shape, 2 * len(pieces))),
        cost_estimate=pl.CostEstimate(
            flops=0, bytes_accessed=4 * len(pieces) * rows * own * half, transcendentals=0
        ),
    )(*pieces, after)


def on_device(image, weight, bias, cotangent):
    n_filt, n_sp = lax.axis_size("filt"), lax.axis_size("sp")
    side_rows = cotangent.shape[0]
    swap = shifted_ring("in", 1)

    gathered = gather_blocks(image)
    taps, bias_col = arrange(weight, bias, image.shape[2], [gathered[-1][0]])
    places = [[(j, k) for j in range(n_sp)] for k in range(n_filt)]
    first, second = places[: n_filt // 2], places[n_filt // 2 :]
    second[-1] = [(0, n_filt - 1)]
    begun = add_blocks(taps, gathered, first[0], side_rows)
    near = send_held(gathered, cotangent, [begun, gathered[0][-2]])
    for group in (sum(first[1:], []), sum(second[:-1], []), second[-1]):
        begun = add_blocks(taps, gathered, group, side_rows, [begun])

    partial = [last_rows(taps, begun, gathered, 0, side_rows)]
    for j in range(1, n_sp):
        partial.append(last_rows(taps, begun, gathered, j, side_rows, [near[j]]))
    other = [lax.ppermute(value, "in", swap) for value in partial]

    own_grad, *rows = silu(partial[0], other[0], bias_col, cotangent, n_filt)
    pieces = rows[:1]
    for k in range(1, n_filt):
        pieces.append(lax.ppermute(rows[k], "filt", shifted_ring("filt", k)))
    others = []
    for j in range(1, n_sp):
        others += [partial[j], other[j], near[j], lax.ppermute(near[j], "in", swap)]
    grad_weight, grad_bias, formed = gradient(bias_col, own_grad, others, gathered)
    output = place_pieces(pieces, formed)
    return (output, grad_weight, grad_bias.reshape(-1))


def solution(mesh):
    placed = (
        P(("groups", "sp", "filt"), None, "in"),
        P(None, None, "filt", None),
        P("filt"),
        P(("groups", "sp"), "filt", None),
    )
    return jax.shard_map(
        on_device,
        mesh=mesh,
        in_specs=placed,
        out_specs=(
            P(("groups", "sp", "filt"), None, "in"),
            P("groups", None, "filt", "in"),
            P(("groups", "filt")),
        ),
        check_vma=False,
    )
```

profile of v0, /device:TPU:0, one launch (start us, length us, event | category | flops | bytes accessed | tf_op | source)
XLA Modules:
  0.0 50.1 jit_solution(7075719680188384146)
XLA Ops:
  0.6 3.1 %collective-permute-start.1 = (bf16[1,256,512]{2,1,0:T(8,128)(2,1)}, bf16[1,256,512]{2,1,0:T(8,128)(2,1)S(1)}, u32[]{:S(2)}, u32[]{:S(2)}) collective-permute-start(bf16[1,256,512]{2,1,0:T(8,128)(2,1)} %refs_4_.1), channel_id=1, source_target_pairs={{0,4},{4,12},{12,8},{8,0},{1,5},{5,13},{13,9},{9,1},{2,6},{6,14},{... | collective-permute-start | bytes 786440 | tf_op jit(solution)/shard_map/ppermute | solution.py:47
  3.7 1.5 %collective-permute-start = (bf16[1,256,512]{2,1,0:T(8,128)(2,1)}, bf16[1,256,512]{2,1,0:T(8,128)(2,1)S(1)}, u32[]{:S(2)}, u32[]{:S(2)}) collective-permute-start(bf16[1,256,512]{2,1,0:T(8,128)(2,1)} %refs_4_.1), channel_id=1, source_target_pairs={{0,2},{2,0},{1,3},{3,1},{4,6},{6,4},{5,7},{7,5},{8,10},{10,8},{9,1... | collective-permute-start | bytes 786440 | tf_op jit(solution)/shard_map/ppermute | solution.py:50
  5.2 6.0 %collective-permute-done.1.refs_1_.refs_5_ = bf16[1,256,512]{2,1,0:T(8,128)(2,1)S(1)} collective-permute-done((bf16[1,256,512]{2,1,0:T(8,128)(2,1)}, bf16[1,256,512]{2,1,0:T(8,128)(2,1)S(1)}, u32[]{:S(2)}, u32[]{:S(2)}) %collective-permute-start.1) | collective-permute-done | bytes 262176 | tf_op jit(solution)/shard_map/ppermute | solution.py:47
  11.2 0.9 %collective-permute-start.3 = (bf16[1,256,512]{2,1,0:T(8,128)(2,1)S(1)}, bf16[1,256,512]{2,1,0:T(8,128)(2,1)S(1)}, u32[]{:S(2)}, u32[]{:S(2)}) collective-permute-start(bf16[1,256,512]{2,1,0:T(8,128)(2,1)S(1)} %collective-permute-done.1.refs_1_.refs_5_), channel_id=1, source_target_pairs={{0,4},{4,12},{12,8},{8,0},{1,5},{5,13},{13,9},{9,1},{2,6},{6,14},{... | collective-permute-start | bytes 786440 | tf_op jit(solution)/shard_map/ppermute | solution.py:47
  12.2 1.5 %collective-permute-start.2 = (bf16[1,256,512]{2,1,0:T(8,128)(2,1)S(1)}, bf16[1,256,512]{2,1,0:T(8,128)(2,1)S(1)}, u32[]{:S(2)}, u32[]{:S(2)}) collective-permute-start(bf16[1,256,512]{2,1,0:T(8,128)(2,1)S(1)} %collective-permute-done.1.refs_1_.refs_5_), channel_id=1, source_target_pairs={{0,2},{2,0},{1,3},{3,1},{4,6},{6,4},{5,7},{7,5},{8,10},{10,8},{9,1... | collective-permute-start | bytes 786440 | tf_op jit(solution)/shard_map/ppermute | solution.py:50
  13.7 0.0 collective-permute-done.refs_0_.refs_1_.refs_8_
  13.7 0.0 copy-start
  13.7 2.3 %copy-done = bf16[3,3,256,1024]{3,2,1,0:T(8,128)(2,1)S(1)} copy-done((bf16[3,3,256,1024]{3,2,1,0:T(8,128)(2,1)S(1)}, bf16[3,3,256,1024]{3,2,1,0:T(8,128)(2,1)}, u32[]{:S(2)}) %copy-start) | copy-done | bytes 4718616
  16.0 0.0 copy-start.2
  16.0 0.7 %copy-done.2 = f32[256]{0:T(256)S(1)} copy-done((f32[256]{0:T(256)S(1)}, f32[256]{0:T(256)}, u32[]{:S(2)}) %copy-start.2) | copy-done | bytes 1048
  16.7 0.0 copy-start.3
  16.7 0.4 shard_map.67
  17.1 2.6 %collective-permute-done.3.refs_1_.refs_2_.refs_6_ = bf16[1,256,512]{2,1,0:T(8,128)(2,1)S(1)} collective-permute-done((bf16[1,256,512]{2,1,0:T(8,128)(2,1)S(1)}, bf16[1,256,512]{2,1,0:T(8,128)(2,1)S(1)}, u32[]{:S(2)}, u32[]{:S(2)}) %collective-permute-start.3) | collective-permute-done | bytes 262176 | tf_op jit(solution)/shard_map/ppermute | solution.py:47
  19.6 0.8 %collective-permute-start.5 = (bf16[1,256,512]{2,1,0:T(8,128)(2,1)S(1)}, bf16[1,256,512]{2,1,0:T(8,128)(2,1)S(1)}, u32[]{:S(2)}, u32[]{:S(2)}) collective-permute-start(bf16[1,256,512]{2,1,0:T(8,128)(2,1)S(1)} %collective-permute-done.3.refs_1_.refs_2_.refs_6_), channel_id=1, source_target_pairs={{0,4},{4,12},{12,8},{8,0},{1,5},{5,13},{13,9},{9,1},{2,6},{6,14},{... | collective-permute-start | bytes 786440 | tf_op jit(solution)/shard_map/ppermute | solution.py:47
  20.4 1.2 %collective-permute-start.4 = (bf16[1,256,512]{2,1,0:T(8,128)(2,1)S(1)}, bf16[1,256,512]{2,1,0:T(8,128)(2,1)S(1)}, u32[]{:S(2)}, u32[]{:S(2)}) collective-permute-start(bf16[1,256,512]{2,1,0:T(8,128)(2,1)S(1)} %collective-permute-done.3.refs_1_.refs_2_.refs_6_), channel_id=1, source_target_pairs={{0,2},{2,0},{1,3},{3,1},{4,6},{6,4},{5,7},{7,5},{8,10},{10,8},{9,1... | collective-permute-start | bytes 786440 | tf_op jit(solution)/shard_map/ppermute | solution.py:50
  21.6 0.0 copy-done.3
  21.6 0.0 copy-start.1
  21.6 1.6 %shard_map.68.refs_0_.refs_1_ = f32[10,256,256]{2,1,0:T(8,128)S(1)} custom-call(bf16[768,1536]{1,0:T(8,128)(2,1)S(1)} %get-tuple-element.15.taps, bf16[1,256,512]{2,1,0:T(8,128)(2,1)S(1)} %copy-done.3, bf16[1,256,512]{2,1,0:T(8,128)(2,1)S(1)} %collective-permute-done.refs_0_.refs_1_.refs_8_), custom_call_target="tpu_custom_call" | custom-call | flops 2013265920 | bytes 1 | tf_op jit(solution)/shard_map/pallas_call | solution.py:188
  23.3 0.0 copy-done.1
  23.3 0.1 shard_map.72
  23.4 2.2 %collective-permute-start.6 = (bf16[1,256,512]{2,1,0:T(8,128)(2,1)S(1)}, bf16[1,256,512]{2,1,0:T(8,128)(2,1)S(1)}, u32[]{:S(2)}, u32[]{:S(2)}) collective-permute-start(bf16[1,256,512]{2,1,0:T(8,128)(2,1)S(1)} %get-tuple-element.16), channel_id=1, source_target_pairs={{0,8},{4,0},{12,4},{8,12},{1,9},{5,1},{13,5},{9,13},{2,10},{6,2},{... | collective-permute-start | bytes 786440 | tf_op jit(solution)/shard_map/ppermute | solution.py:61
  25.6 0.8 %collective-permute-start.11 = (bf16[2,256,256]{2,1,0:T(8,128)(2,1)S(1)}, bf16[2,256,256]{2,1,0:T(8,128)(2,1)S(1)}, u32[]{:S(2)}, u32[]{:S(2)}) collective-permute-start(bf16[2,256,256]{2,1,0:T(8,128)(2,1)S(1)} %get-tuple-element.23), channel_id=1, source_target_pairs={{0,2},{2,0},{1,3},{3,1},{4,6},{6,4},{5,7},{7,5},{8,10},{10,8},{9,1... | collective-permute-start | bytes 786440 | tf_op jit(solution)/shard_map/ppermute | solution.py:62
  26.4 0.0 collective-permute-done.2.refs_2_.refs_9_
  26.4 1.7 %shard_map.69.refs_0_ = f32[10,256,256]{2,1,0:T(8,128)S(1)} custom-call(bf16[768,1536]{1,0:T(8,128)(2,1)S(1)} %get-tuple-element.15.taps, f32[10,256,256]{2,1,0:T(8,128)S(1)} %shard_map.68.refs_0_.refs_1_, bf16[1,256,512]{2,1,0:T(8,128)(2,1)S(1)} %collective-permute-done.1.refs_1_.refs_5_, bf16[1,256,512]{2,1,0:T(8,128)(2,1)S(1)} %collective-permute-done.2.refs_2_.refs_9_), custom_call_target="tpu_custom_call" | custom-call | flops 67108864 | bytes 1 | tf_op jit(solution)/shard_map/pallas_call | solution.py:188
  28.1 0.0 collective-permute-done.4.refs_2_.refs_10_
  28.1 1.7 %shard_map.70.refs_0_ = f32[10,256,256]{2,1,0:T(8,128)S(1)} custom-call(bf16[768,1536]{1,0:T(8,128)(2,1)S(1)} %get-tuple-element.15.taps, f32[10,256,256]{2,1,0:T(8,128)S(1)} %shard_map.69.refs_0_, bf16[1,256,512]{2,1,0:T(8,128)(2,1)S(1)} %collective-permute-done.3.refs_1_.refs_2_.refs_6_, bf16[1,256,512]{2,1,0:T(8,128)(2,1)S(1)} %collective-permute-done.4.refs_2_.refs_10_), custom_call_target="tpu_custom_call" | custom-call | flops 67108864 | bytes 1 | tf_op jit(solution)/shard_map/pallas_call | solution.py:188
  29.8 0.0 collective-permute-done.5.refs_1_.refs_7_
  29.8 1.0 %shard_map.71.begun = f32[10,256,256]{2,1,0:T(8,128)S(1)} custom-call(bf16[768,1536]{1,0:T(8,128)(2,1)S(1)} %get-tuple-element.15.taps, f32[10,256,256]{2,1,0:T(8,128)S(1)} %shard_map.70.refs_0_, bf16[1,256,512]{2,1,0:T(8,128)(2,1)S(1)} %collective-permute-done.5.refs_1_.refs_7_), custom_call_target="tpu_custom_call" | custom-call | flops 33554432 | bytes 1 | tf_op jit(solution)/shard_map/pallas_call | solution.py:188
  30.9 1.8 %collective-permute-done.6.refs_0_.refs_1_.refs_11_ = bf16[1,256,512]{2,1,0:T(8,128)(2,1)S(1)} collective-permute-done((bf16[1,256,512]{2,1,0:T(8,128)(2,1)S(1)}, bf16[1,256,512]{2,1,0:T(8,128)(2,1)S(1)}, u32[]{:S(2)}, u32[]{:S(2)}) %collective-permute-start.6) | collective-permute-done | bytes 262176 | tf_op jit(solution)/shard_map/ppermute | solution.py:61
  32.7 0.1 shard_map.73.mine
  32.9 0.1 collective-permute-start.7
  32.9 0.0 collective-permute-done.11.refs_0_.refs_2_
  33.0 1.0 %shard_map.75.refs_0_ = f32[4,256,256]{2,1,0:T(8,128)S(1)} custom-call(bf16[768,1536]{1,0:T(8,128)(2,1)S(1)} %get-tuple-element.15.taps, f32[10,256,256]{2,1,0:T(8,128)S(1)} %shard_map.71.begun, bf16[2,256,256]{2,1,0:T(8,128)(2,1)S(1)} %collective-permute-done.11.refs_0_.refs_2_, bf16[1,256,512]{2,1,0:T(8,128)(2,1)S(1)} %collective-permute-done.6.refs_0_.refs_1_.refs_11_), custom_call_target="tpu_custom_call" | custom-call | flops 603979776 | bytes 2359296 | tf_op jit(solution)/shard_map/pallas_call | solution.py:239
  34.0 0.6 %collective-permute-start.12 = (f32[4,256,256]{2,1,0:T(8,128)S(1)}, f32[4,256,256]{2,1,0:T(8,128)S(1)}, u32[]{:S(2)}, u32[]{:S(2)}) collective-permute-start(f32[4,256,256]{2,1,0:T(8,128)S(1)} %shard_map.75.refs_0_), channel_id=1, source_target_pairs={{0,1},{1,0},{2,3},{3,2},{4,5},{5,4},{6,7},{7,6},{8,9},{9,8},{10,11... | collective-permute-start | bytes 3145736 | tf_op jit(solution)/shard_map/ppermute | solution.py:463
  34.5 0.1 collective-permute-start.13
  34.6 1.0 %collective-permute-done.7.theirs = f32[4,256,256]{2,1,0:T(8,128)S(1)} collective-permute-done((f32[4,256,256]{2,1,0:T(8,128)S(1)}, f32[4,256,256]{2,1,0:T(8,128)S(1)}, u32[]{:S(2)}, u32[]{:S(2)}) %collective-permute-start.7) | collective-permute-done | bytes 1048608 | tf_op jit(solution)/shard_map/ppermute | solution.py:463
  35.6 0.6 %shard_map.74 = (bf16[4,256,256]{2,1,0:T(8,128)(2,1)S(1)}, bf16[1,256,128]{2,1,0:T(8,128)(2,1)S(1)}, bf16[1,256,128]{2,1,0:T(8,128)(2,1)S(1)}, bf16[1,256,128]{2,1,0:T(8,128)(2,1)S(1)}, bf16[1,256,128]{2,1,0:T(8,128)(2,1)S(1)}) custom-call(f32[4,256,256]{2,1,0:T(8,128)S(1)} %shard_map.73.mine, f32[4,256,256]{2,1,0:T(8,128)S(1)} %collective-permute-done.7.theirs, ...), custom_call_target="tpu_custom_call" | custom-call | flops 2621440 | bytes 3407872 | tf_op jit(solution)/shard_map/pallas_call | solution.py:285
  36.2 2.7 %collective-permute-start.8 = (bf16[1,256,128]{2,1,0:T(8,128)(2,1)S(1)}, bf16[1,256,128]{2,1,0:T(8,128)(2,1)S(1)}, u32[]{:S(2)}, u32[]{:S(2)}) collective-permute-start(bf16[1,256,128]{2,1,0:T(8,128)(2,1)S(1)} %get-tuple-element.19), channel_id=1, source_target_pairs={{0,4},{4,8},{8,12},{12,0},{1,5},{5,9},{9,13},{13,1},{2,6},{6,10},{... | collective-permute-start | bytes 196616 | tf_op jit(solution)/shard_map/ppermute | solution.py:468
  38.8 2.1 %collective-permute-start.9 = (bf16[1,256,128]{2,1,0:T(8,128)(2,1)S(1)}, bf16[1,256,128]{2,1,0:T(8,128)(2,1)S(1)}, u32[]{:S(2)}, u32[]{:S(2)}) collective-permute-start(bf16[1,256,128]{2,1,0:T(8,128)(2,1)S(1)} %get-tuple-element.20), channel_id=1, source_target_pairs={{0,8},{4,12},{8,0},{12,4},{1,9},{5,13},{9,1},{13,5},{2,10},{6,14},... | collective-permute-start | bytes 196616 | tf_op jit(solution)/shard_map/ppermute | solution.py:468
  41.0 0.3 collective-permute-start.10
  41.3 0.0 collective-permute-done.13.refs_3_
  41.3 0.0 collective-permute-done.12.refs_1_
  41.3 7.9 %shard_map.76 = (f32[3,3,256,512]{3,2,1,0:T(8,128)}, f32[1,256]{1,0:T(1,128)}, f32[8,128]{1,0:T(8,128)S(1)}) custom-call(f32[256,1]{1,0:T(8,128)S(1)} %get-tuple-element.17.bias, bf16[4,256,256]{2,1,0:T(8,128)(2,1)S(1)} %get-tuple-element.22.own_grad, f32[4,256,256]{2,1,0:T(8,128)S(1)} %shard_map.75.refs_0_, ...), custom_call_target="tpu_custom_call" | custom-call | flops 4831838208 | bytes 6815744 | tf_op jit(solution)/shard_map/pallas_call | solution.py:389
  49.2 0.0 collective-permute-done.8.refs_1_
  49.2 0.0 collective-permute-done.9.refs_2_
  49.2 0.0 collective-permute-done.10.refs_3_
  49.2 0.7 %shard_map.77 = bf16[1,1024,128]{2,1,0:T(8,128)(2,1)} custom-call(bf16[1,256,128]{2,1,0:T(8,128)(2,1)S(1)} %get-tuple-element.18.refs_0_, bf16[1,256,128]{2,1,0:T(8,128)(2,1)S(1)} %collective-permute-done.8.refs_1_, bf16[1,256,128]{2,1,0:T(8,128)(2,1)S(1)} %collective-permute-done.9.refs_2_, bf16[1,256,128]{2,1,0:T(8,128)(2,1)S(1)} %collective-permute-done.10.refs_3_, ...), custom_call_target="tpu_custom_call" | custom-call | bytes 524288 | tf_op jit(solution)/shard_map/pallas_call | solution.py:432
Async XLA Ops:
  0.6 10.6 %collective-permute-start.1 = (bf16[1,256,512]{2,1,0:T(8,128)(2,1)}, bf16[1,256,512]{2,1,0:T(8,128)(2,1)S(1)}, u32[]{:S(2)}, u32[]{:S(2)}) collective-permute-start(bf16[1,256,512]{2,1,0:T(8,128)(2,1)} %refs_4_.1), channel_id=1, source_target_pairs={{0,4},{4,12},{12,8},{8,0},{1,5},{5,13},{13,9},{9,1},{2,6},{6,14},{... | collective-permute-start | bytes 786440 | tf_op jit(solution)/shard_map/ppermute | solution.py:47
  3.7 10.0 %collective-permute-start = (bf16[1,256,512]{2,1,0:T(8,128)(2,1)}, bf16[1,256,512]{2,1,0:T(8,128)(2,1)S(1)}, u32[]{:S(2)}, u32[]{:S(2)}) collective-permute-start(bf16[1,256,512]{2,1,0:T(8,128)(2,1)} %refs_4_.1), channel_id=1, source_target_pairs={{0,2},{2,0},{1,3},{3,1},{4,6},{6,4},{5,7},{7,5},{8,10},{10,8},{9,1... | collective-permute-start | bytes 786440 | tf_op jit(solution)/shard_map/ppermute | solution.py:50
  11.2 8.4 %collective-permute-start.3 = (bf16[1,256,512]{2,1,0:T(8,128)(2,1)S(1)}, bf16[1,256,512]{2,1,0:T(8,128)(2,1)S(1)}, u32[]{:S(2)}, u32[]{:S(2)}) collective-permute-start(bf16[1,256,512]{2,1,0:T(8,128)(2,1)S(1)} %collective-permute-done.1.refs_1_.refs_5_), channel_id=1, source_target_pairs={{0,4},{4,12},{12,8},{8,0},{1,5},{5,13},{13,9},{9,1},{2,6},{6,14},{... | collective-permute-start | bytes 786440 | tf_op jit(solution)/shard_map/ppermute | solution.py:47
  12.2 14.2 %collective-permute-start.2 = (bf16[1,256,512]{2,1,0:T(8,128)(2,1)S(1)}, bf16[1,256,512]{2,1,0:T(8,128)(2,1)S(1)}, u32[]{:S(2)}, u32[]{:S(2)}) collective-permute-start(bf16[1,256,512]{2,1,0:T(8,128)(2,1)S(1)} %collective-permute-done.1.refs_1_.refs_5_), channel_id=1, source_target_pairs={{0,2},{2,0},{1,3},{3,1},{4,6},{6,4},{5,7},{7,5},{8,10},{10,8},{9,1... | collective-permute-start | bytes 786440 | tf_op jit(solution)/shard_map/ppermute | solution.py:50
  13.7 2.3 %copy-start = (bf16[3,3,256,1024]{3,2,1,0:T(8,128)(2,1)S(1)}, bf16[3,3,256,1024]{3,2,1,0:T(8,128)(2,1)}, u32[]{:S(2)}) copy-start(bf16[3,3,256,1024]{3,2,1,0:T(8,128)(2,1)} %weight.1) | copy-start | bytes 14155780
  16.0 0.7 %copy-start.2 = (f32[256]{0:T(256)S(1)}, f32[256]{0:T(256)}, u32[]{:S(2)}) copy-start(f32[256]{0:T(256)} %param.6) | copy-start | bytes 3076
  16.7 4.9 %copy-start.3 = (bf16[1,256,512]{2,1,0:T(8,128)(2,1)S(1)}, bf16[1,256,512]{2,1,0:T(8,128)(2,1)}, u32[]{:S(2)}) copy-start(bf16[1,256,512]{2,1,0:T(8,128)(2,1)} %refs_4_.1) | copy-start | bytes 786436
  19.6 10.2 %collective-permute-start.5 = (bf16[1,256,512]{2,1,0:T(8,128)(2,1)S(1)}, bf16[1,256,512]{2,1,0:T(8,128)(2,1)S(1)}, u32[]{:S(2)}, u32[]{:S(2)}) collective-permute-start(bf16[1,256,512]{2,1,0:T(8,128)(2,1)S(1)} %collective-permute-done.3.refs_1_.refs_2_.refs_6_), channel_id=1, source_target_pairs={{0,4},{4,12},{12,8},{8,0},{1,5},{5,13},{13,9},{9,1},{2,6},{6,14},{... | collective-permute-start | bytes 786440 | tf_op jit(solution)/shard_map/ppermute | solution.py:47
  20.4 7.7 %collective-permute-start.4 = (bf16[1,256,512]{2,1,0:T(8,128)(2,1)S(1)}, bf16[1,256,512]{2,1,0:T(8,128)(2,1)S(1)}, u32[]{:S(2)}, u32[]{:S(2)}) collective-permute-start(bf16[1,256,512]{2,1,0:T(8,128)(2,1)S(1)} %collective-permute-done.3.refs_1_.refs_2_.refs_6_), channel_id=1, source_target_pairs={{0,2},{2,0},{1,3},{3,1},{4,6},{6,4},{5,7},{7,5},{8,10},{10,8},{9,1... | collective-permute-start | bytes 786440 | tf_op jit(solution)/shard_map/ppermute | solution.py:50
  21.6 1.6 %copy-start.1 = (bf16[4,256,256]{2,1,0:T(8,128)(2,1)S(1)}, bf16[4,256,256]{2,1,0:T(8,128)(2,1)}, u32[]{:S(2)}) copy-start(bf16[4,256,256]{2,1,0:T(8,128)(2,1)} %cotangent.3) | copy-start | bytes 1572868
  23.4 9.3 %collective-permute-start.6 = (bf16[1,256,512]{2,1,0:T(8,128)(2,1)S(1)}, bf16[1,256,512]{2,1,0:T(8,128)(2,1)S(1)}, u32[]{:S(2)}, u32[]{:S(2)}) collective-permute-start(bf16[1,256,512]{2,1,0:T(8,128)(2,1)S(1)} %get-tuple-element.16), channel_id=1, source_target_pairs={{0,8},{4,0},{12,4},{8,12},{1,9},{5,1},{13,5},{9,13},{2,10},{6,2},{... | collective-permute-start | bytes 786440 | tf_op jit(solution)/shard_map/ppermute | solution.py:61
  25.6 7.4 %collective-permute-start.11 = (bf16[2,256,256]{2,1,0:T(8,128)(2,1)S(1)}, bf16[2,256,256]{2,1,0:T(8,128)(2,1)S(1)}, u32[]{:S(2)}, u32[]{:S(2)}) collective-permute-start(bf16[2,256,256]{2,1,0:T(8,128)(2,1)S(1)} %get-tuple-element.23), channel_id=1, source_target_pairs={{0,2},{2,0},{1,3},{3,1},{4,6},{6,4},{5,7},{7,5},{8,10},{10,8},{9,1... | collective-permute-start | bytes 786440 | tf_op jit(solution)/shard_map/ppermute | solution.py:62
  32.9 2.7 %collective-permute-start.7 = (f32[4,256,256]{2,1,0:T(8,128)S(1)}, f32[4,256,256]{2,1,0:T(8,128)S(1)}, u32[]{:S(2)}, u32[]{:S(2)}) collective-permute-start(f32[4,256,256]{2,1,0:T(8,128)S(1)} %shard_map.73.mine), channel_id=1, source_target_pairs={{0,1},{1,0},{2,3},{3,2},{4,5},{5,4},{6,7},{7,6},{8,9},{9,8},{10,11... | collective-permute-start | bytes 3145736 | tf_op jit(solution)/shard_map/ppermute | solution.py:463
  34.0 7.3 %collective-permute-start.12 = (f32[4,256,256]{2,1,0:T(8,128)S(1)}, f32[4,256,256]{2,1,0:T(8,128)S(1)}, u32[]{:S(2)}, u32[]{:S(2)}) collective-permute-start(f32[4,256,256]{2,1,0:T(8,128)S(1)} %shard_map.75.refs_0_), channel_id=1, source_target_pairs={{0,1},{1,0},{2,3},{3,2},{4,5},{5,4},{6,7},{7,6},{8,9},{9,8},{10,11... | collective-permute-start | bytes 3145736 | tf_op jit(solution)/shard_map/ppermute | solution.py:463
  34.5 6.8 %collective-permute-start.13 = (bf16[2,256,256]{2,1,0:T(8,128)(2,1)S(1)}, bf16[2,256,256]{2,1,0:T(8,128)(2,1)S(1)}, u32[]{:S(2)}, u32[]{:S(2)}) collective-permute-start(bf16[2,256,256]{2,1,0:T(8,128)(2,1)S(1)} %collective-permute-done.11.refs_0_.refs_2_), channel_id=1, source_target_pairs={{0,1},{1,0},{2,3},{3,2},{4,5},{5,4},{6,7},{7,6},{8,9},{9,8},{10,11... | collective-permute-start | bytes 786440 | tf_op jit(solution)/shard_map/ppermute | solution.py:471
  36.2 13.0 %collective-permute-start.8 = (bf16[1,256,128]{2,1,0:T(8,128)(2,1)S(1)}, bf16[1,256,128]{2,1,0:T(8,128)(2,1)S(1)}, u32[]{:S(2)}, u32[]{:S(2)}) collective-permute-start(bf16[1,256,128]{2,1,0:T(8,128)(2,1)S(1)} %get-tuple-element.19), channel_id=1, source_target_pairs={{0,4},{4,8},{8,12},{12,0},{1,5},{5,9},{9,13},{13,1},{2,6},{6,10},{... | collective-permute-start | bytes 196616 | tf_op jit(solution)/shard_map/ppermute | solution.py:468
  38.8 10.3 %collective-permute-start.9 = (bf16[1,256,128]{2,1,0:T(8,128)(2,1)S(1)}, bf16[1,256,128]{2,1,0:T(8,128)(2,1)S(1)}, u32[]{:S(2)}, u32[]{:S(2)}) collective-permute-start(bf16[1,256,128]{2,1,0:T(8,128)(2,1)S(1)} %get-tuple-element.20), channel_id=1, source_target_pairs={{0,8},{4,12},{8,0},{12,4},{1,9},{5,13},{9,1},{13,5},{2,10},{6,14},... | collective-permute-start | bytes 196616 | tf_op jit(solution)/shard_map/ppermute | solution.py:468
  41.0 8.2 %collective-permute-start.10 = (bf16[1,256,128]{2,1,0:T(8,128)(2,1)S(1)}, bf16[1,256,128]{2,1,0:T(8,128)(2,1)S(1)}, u32[]{:S(2)}, u32[]{:S(2)}) collective-permute-start(bf16[1,256,128]{2,1,0:T(8,128)(2,1)S(1)} %get-tuple-element.21), channel_id=1, source_target_pairs={{0,12},{4,0},{8,4},{12,8},{1,13},{5,1},{9,5},{13,9},{2,14},{6,2},{... | collective-permute-start | bytes 196616 | tf_op jit(solution)/shard_map/ppermute | solution.py:468
where the time goes:
time: 50.3 us; the launch traced here: 50.1 us
  starting transfers between devices  17.8 us (35%)
  Pallas kernels  16.8 us (33%)
  waiting for transfers between devices  11.5 us (23%)
  local copies, waits for them, and re-layouts  3.02 us (6%)
  between operations  0.94 us (2%)
    ppermute x3, waiting for transfers between devices, gather_blocks(): blocks[0][k] = lax.ppermute(blocks[0][k - 1], 'filt', outward)  8.61 us
    pallas_call x1, Pallas kernels, gradient(): pl.pallas_call(functools.partial(gradient_kernel, n_filt, n_sp), out_shap...  7.87 us
    pallas_call x4, Pallas kernels, add_blocks(): pl.pallas_call(functools.partial(add_blocks_kernel, where, n_filt, n_sp,...  6.05 us
    ppermute x3, starting transfers between devices, on_device(): pieces.append(lax.ppermute(rows[k], 'filt', shifted_ring('filt', k)))  5.12 us
    ppermute x3, starting transfers between devices, gather_blocks(): blocks[0][k] = lax.ppermute(blocks[0][k - 1], 'filt', outward)  4.78 us
    ppermute x3, starting transfers between devices, gather_blocks(): blocks[j][k] = lax.ppermute(blocks[j - 1][k], 'sp', onward)  4.23 us
    unnamed x8, local copies, waits for them, and re-layouts  3.02 us
    ppermute x1, starting transfers between devices, send_held(): blocks[j][-1] = lax.ppermute(first[j - 1], 'filt', folded_ring('filt', -1))  2.19 us
  transfers between devices with their start and end apart: 14, of which 4 were waited for; matrix products, arithmetic and copies ran while one was open for 0% of the time, Pallas kernels for 32%

commit v1 on v0

--- a/solution.py
+++ b/solution.py
@@ -200,12 +200,47 @@
     )(taps, *begun, *blocks)
 
 
-def last_rows_kernel(n_filt, n_sp, j, n_after, taps, begun, *refs):
+def row_terms_kernel(taps, block, _, terms, turned):
+    own = taps.shape[0] // 3
+    for i in range(block.shape[0]):
+        turn_row(turned.at[i], block[i])
+        product = jnp.dot(taps[...], turned[i], preferred_element_type=jnp.float32)
+        for a in range(3):
+            terms[i, a] = product[a * own : (a + 1) * own]
+
+
+def row_terms(taps, block, after):
+    rows_dev, width, depth = block.shape
+    own = taps.shape[0] // 3
+    shape = (rows_dev, 3, own, width)
+    turned = (rows_dev, 3 * depth, width)
+    return pl.pallas_call(
+        row_terms_kernel,
+        out_shape=jax.ShapeDtypeStruct(shape, jnp.float32),
+        in_specs=[VMEM, VMEM, ANY],
+        out_specs=VMEM,
+        scratch_shapes=[pltpu.VMEM(turned, block.dtype)],
+        compiler_params=params((turned, 3), (shape, 8), (taps.shape, 4)),
+        cost_estimate=pl.CostEstimate(
+            flops=18 * rows_dev * own * width * depth, bytes_accessed=1, transcendentals=0
+        ),
+    )(taps, block, after)
+
+
+def last_rows_kernel(n_filt, n_sp, j, n_after, taps, begun, terms, *refs):
     *blocks, out, total, turned = refs[n_after:]
     rows_dev = blocks[0].shape[0]
     side_rows, own = total.shape[0] - 2, total.shape[1]
     side = behind("sp", n_sp, j)
     total[...] = begun[pl.ds(side * side_rows, side_rows + 2)]
+    first = block_place(n_filt - 1, n_filt, n_sp) * rows_dev - side * side_rows + 1
+    for i in range(rows_dev):
+        for a in range(3):
+            slot = first + i + 1 - a
+
+            @pl.when((slot >= 0) & (slot < side_rows + 2))
+            def _():
+                total[slot] += terms[i, a]
 
     def slot_of(other):
         place = block_place(other * n_filt + n_filt - 1, n_filt, n_sp)
@@ -228,7 +263,7 @@
     out[...] = total[pl.ds(1, side_rows)]
 
 
-def last_rows(taps, begun, sides, j, side_rows, after=()):
+def last_rows(taps, begun, terms, sides, j, side_rows, after=()):
     n_sp, n_filt = len(sides), len(sides[0])
     blocks = [side[-1] for side in sides[1:]]
     rows_dev, width, depth = blocks[0].shape
@@ -239,21 +274,21 @@
     return pl.pallas_call(
         functools.partial(last_rows_kernel, n_filt, n_sp, j, len(after)),
         out_shape=jax.ShapeDtypeStruct(out, jnp.float32),
-        in_specs=[VMEM] * 2 + [ANY] * len(after) + [VMEM] * len(blocks),
+        in_specs=[VMEM] * 3 + [ANY] * len(after) + [VMEM] * len(blocks),
         out_specs=VMEM,
         scratch_shapes=[
             pltpu.VMEM(total, jnp.float32),
             pltpu.VMEM(turned, blocks[0].dtype),
         ],
         compiler_params=params(
-            (turned, 2 + n_sp), (total, 12), (begun.shape, 4), (taps.shape, 4)
+            (turned, 2 + n_sp), (total, 12), (begun.shape, 4), (taps.shape, 4), (terms.shape, 4)
         ),
         cost_estimate=pl.CostEstimate(
             flops=18 * rows_dev * own * width * depth,
             bytes_accessed=18 * own * depth,
             transcendentals=0,
         ),
-    )(taps, begun, *after, *blocks)
+    )(taps, begun, terms, *after, *blocks)
 
 
 def silu_parts(shifted, cotangent):
@@ -343,8 +378,7 @@
     def copy_out(a, b):
         return pltpu.make_async_copy(stage.at[a, b], weight_sum.at[a, b], sems.at[a, b])
 
-    for a in range(3):
-        stage[a] = tap_gradient(0, a).reshape(stage.shape[1:])
+    stage[0] = tap_gradient(0, 0).reshape(stage.shape[1:])
     for j in range(1, n_sp):
         mine, theirs, near, far = others[4 * (j - 1) : 4 * j]
         for h, cotangent in enumerate((near, far)):
@@ -355,12 +389,13 @@
                 shift_grads(grads[j], grad_out, start + r)
 
     for a in range(3):
-        for j in range(1, n_sp):
-            product = tap_gradient(j, a)
-            for b in range(3):
-                stage[a, b] += product[b * own : (b + 1) * own]
-                if j == n_sp - 1:
-                    copy_out(a, b).start()
+        product = tap_gradient(1, a)
+        for j in [*([0] if a else []), *range(2, n_sp)]:
+            product += tap_gradient(j, a)
+        for b in range(3):
+            term = product[b * own : (b + 1) * own]
+            stage[a, b] = term if a else stage[a, b] + term
+            copy_out(a, b).start()
 
     total = jnp.zeros((16, own), jnp.float32)
     for side in grads:
@@ -451,15 +486,15 @@
     taps, bias_col = arrange(weight, bias, image.shape[2], [gathered[-1][0]])
     places = [[(j, k) for j in range(n_sp)] for k in range(n_filt)]
     first, second = places[: n_filt // 2], places[n_filt // 2 :]
-    second[-1] = [(0, n_filt - 1)]
     begun = add_blocks(taps, gathered, first[0], side_rows)
     near = send_held(gathered, cotangent, [begun, gathered[0][-2]])
-    for group in (sum(first[1:], []), sum(second[:-1], []), second[-1]):
+    for group in (sum(first[1:], []), sum(second[:-1], [])):
         begun = add_blocks(taps, gathered, group, side_rows, [begun])
 
-    partial = [last_rows(taps, begun, gathered, 0, side_rows)]
+    terms = row_terms(taps, gathered[0][-1], begun)
+    partial = [last_rows(taps, begun, terms, gathered, 0, side_rows)]
     for j in range(1, n_sp):
-        partial.append(last_rows(taps, begun, gathered, j, side_rows, [near[j]]))
+        partial.append(last_rows(taps, begun, terms, gathered, j, side_rows, [near[j]]))
     other = [lax.ppermute(value, "in", swap) for value in partial]
 
     own_grad, *rows = silu(partial[0], other[0], bias_col, cotangent, n_filt)

time: 50.3 us -> 50.3 us (level)
    pallas_call x4 -> x3, Pallas kernels: 6.05 us -> 5.04 us  [add_blocks(): pl.pallas_call(functools.partial(add_blocks_kernel, where, n_filt, n_sp,...]
    pallas_call x0 -> x1, Pallas kernels: none -> 0.93 us  [row_terms(): pl.pallas_call(row_terms_kernel, out_shape=jax.ShapeDtypeStruct(shape, jn...]
where the time goes in v1:
time: 50.3 us; the launch traced here: 50.1 us
  starting transfers between devices  17.7 us (35%)
  Pallas kernels  16.9 us (34%)
  waiting for transfers between devices  11.5 us (23%)
  local copies, waits for them, and re-layouts  3.02 us (6%)
  between operations  0.94 us (2%)
    ppermute x3, waiting for transfers between devices, gather_blocks(): blocks[0][k] = lax.ppermute(blocks[0][k - 1], 'filt', outward)  8.61 us
    pallas_call x1, Pallas kernels, gradient(): pl.pallas_call(functools.partial(gradient_kernel, n_filt, n_sp), out_shap...  7.86 us
    pallas_call x3, Pallas kernels, add_blocks(): pl.pallas_call(functools.partial(add_blocks_kernel, where, n_filt, n_sp,...  5.04 us
    ppermute x3, starting transfers between devices, on_device(): pieces.append(lax.ppermute(rows[k], 'filt', shifted_ring('filt', k)))  5.03 us
    ppermute x3, starting transfers between devices, gather_blocks(): blocks[0][k] = lax.ppermute(blocks[0][k - 1], 'filt', outward)  4.78 us
    ppermute x3, starting transfers between devices, gather_blocks(): blocks[j][k] = lax.ppermute(blocks[j - 1][k], 'sp', onward)  4.23 us
    unnamed x8, local copies, waits for them, and re-layouts  3.02 us
    ppermute x1, starting transfers between devices, send_held(): blocks[j][-1] = lax.ppermute(first[j - 1], 'filt', folded_ring('filt', -1))  2.19 us
  transfers between devices with their start and end apart: 14, of which 4 were waited for; matrix products, arithmetic and copies ran while one was open for 0% of the time, Pallas kernels for 32%

profile of v1, /device:TPU:0, one launch (start us, length us, event | category | flops | bytes accessed | tf_op | source)
XLA Modules:
  0.0 50.1 jit_solution(11765631344691083986)
XLA Ops:
  0.6 3.1 %collective-permute-start.1 = (bf16[1,256,512]{2,1,0:T(8,128)(2,1)}, bf16[1,256,512]{2,1,0:T(8,128)(2,1)S(1)}, u32[]{:S(2)}, u32[]{:S(2)}) collective-permute-start(bf16[1,256,512]{2,1,0:T(8,128)(2,1)} %refs_4_.1), channel_id=1, source_target_pairs={{0,4},{4,12},{12,8},{8,0},{1,5},{5,13},{13,9},{9,1},{2,6},{6,14},{... | collective-permute-start | bytes 786440 | tf_op jit(solution)/shard_map/ppermute | solution.py:47
  3.7 1.5 %collective-permute-start = (bf16[1,256,512]{2,1,0:T(8,128)(2,1)}, bf16[1,256,512]{2,1,0:T(8,128)(2,1)S(1)}, u32[]{:S(2)}, u32[]{:S(2)}) collective-permute-start(bf16[1,256,512]{2,1,0:T(8,128)(2,1)} %refs_4_.1), channel_id=1, source_target_pairs={{0,2},{2,0},{1,3},{3,1},{4,6},{6,4},{5,7},{7,5},{8,10},{10,8},{9,1... | collective-permute-start | bytes 786440 | tf_op jit(solution)/shard_map/ppermute | solution.py:50
  5.2 6.0 %collective-permute-done.1.refs_1_.refs_5_ = bf16[1,256,512]{2,1,0:T(8,128)(2,1)S(1)} collective-permute-done((bf16[1,256,512]{2,1,0:T(8,128)(2,1)}, bf16[1,256,512]{2,1,0:T(8,128)(2,1)S(1)}, u32[]{:S(2)}, u32[]{:S(2)}) %collective-permute-start.1) | collective-permute-done | bytes 262176 | tf_op jit(solution)/shard_map/ppermute | solution.py:47
  11.2 0.9 %collective-permute-start.3 = (bf16[1,256,512]{2,1,0:T(8,128)(2,1)S(1)}, bf16[1,256,512]{2,1,0:T(8,128)(2,1)S(1)}, u32[]{:S(2)}, u32[]{:S(2)}) collective-permute-start(bf16[1,256,512]{2,1,0:T(8,128)(2,1)S(1)} %collective-permute-done.1.refs_1_.refs_5_), channel_id=1, source_target_pairs={{0,4},{4,12},{12,8},{8,0},{1,5},{5,13},{13,9},{9,1},{2,6},{6,14},{... | collective-permute-start | bytes 786440 | tf_op jit(solution)/shard_map/ppermute | solution.py:47
  12.2 1.5 %collective-permute-start.2 = (bf16[1,256,512]{2,1,0:T(8,128)(2,1)S(1)}, bf16[1,256,512]{2,1,0:T(8,128)(2,1)S(1)}, u32[]{:S(2)}, u32[]{:S(2)}) collective-permute-start(bf16[1,256,512]{2,1,0:T(8,128)(2,1)S(1)} %collective-permute-done.1.refs_1_.refs_5_), channel_id=1, source_target_pairs={{0,2},{2,0},{1,3},{3,1},{4,6},{6,4},{5,7},{7,5},{8,10},{10,8},{9,1... | collective-permute-start | bytes 786440 | tf_op jit(solution)/shard_map/ppermute | solution.py:50
  13.7 0.0 collective-permute-done.refs_0_.refs_1_.refs_8_
  13.7 0.0 copy-start
  13.7 2.3 %copy-done = bf16[3,3,256,1024]{3,2,1,0:T(8,128)(2,1)S(1)} copy-done((bf16[3,3,256,1024]{3,2,1,0:T(8,128)(2,1)S(1)}, bf16[3,3,256,1024]{3,2,1,0:T(8,128)(2,1)}, u32[]{:S(2)}) %copy-start) | copy-done | bytes 4718616
  16.0 0.0 copy-start.2
  16.0 0.7 %copy-done.2 = f32[256]{0:T(256)S(1)} copy-done((f32[256]{0:T(256)S(1)}, f32[256]{0:T(256)}, u32[]{:S(2)}) %copy-start.2) | copy-done | bytes 1048
  16.7 0.0 copy-start.3
  16.7 0.4 shard_map.67
  17.1 2.6 %collective-permute-done.3.refs_1_.refs_2_.refs_6_ = bf16[1,256,512]{2,1,0:T(8,128)(2,1)S(1)} collective-permute-done((bf16[1,256,512]{2,1,0:T(8,128)(2,1)S(1)}, bf16[1,256,512]{2,1,0:T(8,128)(2,1)S(1)}, u32[]{:S(2)}, u32[]{:S(2)}) %collective-permute-start.3) | collective-permute-done | bytes 262176 | tf_op jit(solution)/shard_map/ppermute | solution.py:47
  19.6 0.8 %collective-permute-start.5 = (bf16[1,256,512]{2,1,0:T(8,128)(2,1)S(1)}, bf16[1,256,512]{2,1,0:T(8,128)(2,1)S(1)}, u32[]{:S(2)}, u32[]{:S(2)}) collective-permute-start(bf16[1,256,512]{2,1,0:T(8,128)(2,1)S(1)} %collective-permute-done.3.refs_1_.refs_2_.refs_6_), channel_id=1, source_target_pairs={{0,4},{4,12},{12,8},{8,0},{1,5},{5,13},{13,9},{9,1},{2,6},{6,14},{... | collective-permute-start | bytes 786440 | tf_op jit(solution)/shard_map/ppermute | solution.py:47
  20.4 1.2 %collective-permute-start.4 = (bf16[1,256,512]{2,1,0:T(8,128)(2,1)S(1)}, bf16[1,256,512]{2,1,0:T(8,128)(2,1)S(1)}, u32[]{:S(2)}, u32[]{:S(2)}) collective-permute-start(bf16[1,256,512]{2,1,0:T(8,128)(2,1)S(1)} %collective-permute-done.3.refs_1_.refs_2_.refs_6_), channel_id=1, source_target_pairs={{0,2},{2,0},{1,3},{3,1},{4,6},{6,4},{5,7},{7,5},{8,10},{10,8},{9,1... | collective-permute-start | bytes 786440 | tf_op jit(solution)/shard_map/ppermute | solution.py:50
  21.6 0.0 copy-done.3
  21.6 0.0 copy-start.1
  21.6 1.6 %shard_map.68.refs_0_.refs_1_ = f32[10,256,256]{2,1,0:T(8,128)S(1)} custom-call(bf16[768,1536]{1,0:T(8,128)(2,1)S(1)} %get-tuple-element.15.taps, bf16[1,256,512]{2,1,0:T(8,128)(2,1)S(1)} %copy-done.3, bf16[1,256,512]{2,1,0:T(8,128)(2,1)S(1)} %collective-permute-done.refs_0_.refs_1_.refs_8_), custom_call_target="tpu_custom_call" | custom-call | flops 2013265920 | bytes 1 | tf_op jit(solution)/shard_map/pallas_call | solution.py:188
  23.3 0.0 copy-done.1
  23.3 0.1 shard_map.72
  23.4 2.2 %collective-permute-start.6 = (bf16[1,256,512]{2,1,0:T(8,128)(2,1)S(1)}, bf16[1,256,512]{2,1,0:T(8,128)(2,1)S(1)}, u32[]{:S(2)}, u32[]{:S(2)}) collective-permute-start(bf16[1,256,512]{2,1,0:T(8,128)(2,1)S(1)} %get-tuple-element.16), channel_id=1, source_target_pairs={{0,8},{4,0},{12,4},{8,12},{1,9},{5,1},{13,5},{9,13},{2,10},{6,2},{... | collective-permute-start | bytes 786440 | tf_op jit(solution)/shard_map/ppermute | solution.py:61
  25.6 0.8 %collective-permute-start.11 = (bf16[2,256,256]{2,1,0:T(8,128)(2,1)S(1)}, bf16[2,256,256]{2,1,0:T(8,128)(2,1)S(1)}, u32[]{:S(2)}, u32[]{:S(2)}) collective-permute-start(bf16[2,256,256]{2,1,0:T(8,128)(2,1)S(1)} %get-tuple-element.23), channel_id=1, source_target_pairs={{0,2},{2,0},{1,3},{3,1},{4,6},{6,4},{5,7},{7,5},{8,10},{10,8},{9,1... | collective-permute-start | bytes 786440 | tf_op jit(solution)/shard_map/ppermute | solution.py:62
  26.4 0.0 collective-permute-done.2.refs_2_.refs_9_
  26.4 1.7 %shard_map.69.refs_0_ = f32[10,256,256]{2,1,0:T(8,128)S(1)} custom-call(bf16[768,1536]{1,0:T(8,128)(2,1)S(1)} %get-tuple-element.15.taps, f32[10,256,256]{2,1,0:T(8,128)S(1)} %shard_map.68.refs_0_.refs_1_, bf16[1,256,512]{2,1,0:T(8,128)(2,1)S(1)} %collective-permute-done.1.refs_1_.refs_5_, bf16[1,256,512]{2,1,0:T(8,128)(2,1)S(1)} %collective-permute-done.2.refs_2_.refs_9_), custom_call_target="tpu_custom_call" | custom-call | flops 67108864 | bytes 1 | tf_op jit(solution)/shard_map/pallas_call | solution.py:188
  28.1 0.0 collective-permute-done.4.refs_2_.refs_10_
  28.1 1.7 %shard_map.70._.begun = f32[10,256,256]{2,1,0:T(8,128)S(1)} custom-call(bf16[768,1536]{1,0:T(8,128)(2,1)S(1)} %get-tuple-element.15.taps, f32[10,256,256]{2,1,0:T(8,128)S(1)} %shard_map.69.refs_0_, bf16[1,256,512]{2,1,0:T(8,128)(2,1)S(1)} %collective-permute-done.3.refs_1_.refs_2_.refs_6_, bf16[1,256,512]{2,1,0:T(8,128)(2,1)S(1)} %collective-permute-done.4.refs_2_.refs_10_), custom_call_target="tpu_custom_call" | custom-call | flops 67108864 | bytes 1 | tf_op jit(solution)/shard_map/pallas_call | solution.py:188
  29.8 0.0 collective-permute-done.5.block.refs_7_
  29.8 0.9 %shard_map.71.terms = f32[1,3,256,256]{3,2,1,0:T(8,128)S(1)} custom-call(bf16[768,1536]{1,0:T(8,128)(2,1)S(1)} %get-tuple-element.15.taps, bf16[1,256,512]{2,1,0:T(8,128)(2,1)S(1)} %collective-permute-done.5.block.refs_7_, f32[10,256,256]{2,1,0:T(8,128)S(1)} %shard_map.70._.begun), custom_call_target="tpu_custom_call" | custom-call | flops 603979776 | bytes 1 | tf_op jit(solution)/shard_map/pallas_call | solution.py:217
  30.8 1.9 %collective-permute-done.6.refs_0_.refs_1_.refs_11_ = bf16[1,256,512]{2,1,0:T(8,128)(2,1)S(1)} collective-permute-done((bf16[1,256,512]{2,1,0:T(8,128)(2,1)S(1)}, bf16[1,256,512]{2,1,0:T(8,128)(2,1)S(1)}, u32[]{:S(2)}, u32[]{:S(2)}) %collective-permute-start.6) | collective-permute-done | bytes 262176 | tf_op jit(solution)/shard_map/ppermute | solution.py:61
  32.7 0.3 shard_map.73.mine
  33.0 0.1 collective-permute-start.7
  33.1 0.0 collective-permute-done.11.refs_0_.refs_2_
  33.1 1.1 %shard_map.75.refs_0_ = f32[4,256,256]{2,1,0:T(8,128)S(1)} custom-call(bf16[768,1536]{1,0:T(8,128)(2,1)S(1)} %get-tuple-element.15.taps, f32[10,256,256]{2,1,0:T(8,128)S(1)} %shard_map.70._.begun, f32[1,3,256,256]{3,2,1,0:T(8,128)S(1)} %shard_map.71.terms, bf16[2,256,256]{2,1,0:T(8,128)(2,1)S(1)} %collective-permute-done.11.refs_0_.refs_2_, ...), custom_call_target="tpu_custom_call" | custom-call | flops 603979776 | bytes 2359296 | tf_op jit(solution)/shard_map/pallas_call | solution.py:274
  34.2 0.5 %collective-permute-start.12 = (f32[4,256,256]{2,1,0:T(8,128)S(1)}, f32[4,256,256]{2,1,0:T(8,128)S(1)}, u32[]{:S(2)}, u32[]{:S(2)}) collective-permute-start(f32[4,256,256]{2,1,0:T(8,128)S(1)} %shard_map.75.refs_0_), channel_id=1, source_target_pairs={{0,1},{1,0},{2,3},{3,2},{4,5},{5,4},{6,7},{7,6},{8,9},{9,8},{10,11... | collective-permute-start | bytes 3145736 | tf_op jit(solution)/shard_map/ppermute | solution.py:498
  34.8 0.1 collective-permute-start.13
  34.8 0.9 %collective-permute-done.7.theirs = f32[4,256,256]{2,1,0:T(8,128)S(1)} collective-permute-done((f32[4,256,256]{2,1,0:T(8,128)S(1)}, f32[4,256,256]{2,1,0:T(8,128)S(1)}, u32[]{:S(2)}, u32[]{:S(2)}) %collective-permute-start.7) | collective-permute-done | bytes 1048608 | tf_op jit(solution)/shard_map/ppermute | solution.py:498
  35.7 0.6 %shard_map.74 = (bf16[4,256,256]{2,1,0:T(8,128)(2,1)S(1)}, bf16[1,256,128]{2,1,0:T(8,128)(2,1)S(1)}, bf16[1,256,128]{2,1,0:T(8,128)(2,1)S(1)}, bf16[1,256,128]{2,1,0:T(8,128)(2,1)S(1)}, bf16[1,256,128]{2,1,0:T(8,128)(2,1)S(1)}) custom-call(f32[4,256,256]{2,1,0:T(8,128)S(1)} %shard_map.73.mine, f32[4,256,256]{2,1,0:T(8,128)S(1)} %collective-permute-done.7.theirs, ...), custom_call_target="tpu_custom_call" | custom-call | flops 2621440 | bytes 3407872 | tf_op jit(solution)/shard_map/pallas_call | solution.py:320
  36.3 2.6 %collective-permute-start.8 = (bf16[1,256,128]{2,1,0:T(8,128)(2,1)S(1)}, bf16[1,256,128]{2,1,0:T(8,128)(2,1)S(1)}, u32[]{:S(2)}, u32[]{:S(2)}) collective-permute-start(bf16[1,256,128]{2,1,0:T(8,128)(2,1)S(1)} %get-tuple-element.19), channel_id=1, source_target_pairs={{0,4},{4,8},{8,12},{12,0},{1,5},{5,9},{9,13},{13,1},{2,6},{6,10},{... | collective-permute-start | bytes 196616 | tf_op jit(solution)/shard_map/ppermute | solution.py:503
  38.9 2.1 %collective-permute-start.9 = (bf16[1,256,128]{2,1,0:T(8,128)(2,1)S(1)}, bf16[1,256,128]{2,1,0:T(8,128)(2,1)S(1)}, u32[]{:S(2)}, u32[]{:S(2)}) collective-permute-start(bf16[1,256,128]{2,1,0:T(8,128)(2,1)S(1)} %get-tuple-element.20), channel_id=1, source_target_pairs={{0,8},{4,12},{8,0},{12,4},{1,9},{5,13},{9,1},{13,5},{2,10},{6,14},... | collective-permute-start | bytes 196616 | tf_op jit(solution)/shard_map/ppermute | solution.py:503
  41.0 0.3 collective-permute-start.10
  41.3 0.0 collective-permute-done.13.refs_3_
  41.3 0.0 collective-permute-done.12.refs_1_
  41.3 7.9 %shard_map.76 = (f32[3,3,256,512]{3,2,1,0:T(8,128)}, f32[1,256]{1,0:T(1,128)}, f32[8,128]{1,0:T(8,128)S(1)}) custom-call(f32[256,1]{1,0:T(8,128)S(1)} %get-tuple-element.17.bias, bf16[4,256,256]{2,1,0:T(8,128)(2,1)S(1)} %get-tuple-element.22.own_grad, f32[4,256,256]{2,1,0:T(8,128)S(1)} %shard_map.75.refs_0_, ...), custom_call_target="tpu_custom_call" | custom-call | flops 4831838208 | bytes 6815744 | tf_op jit(solution)/shard_map/pallas_call | solution.py:424
  49.2 0.0 collective-permute-done.8.refs_1_
  49.2 0.0 collective-permute-done.9.refs_2_
  49.2 0.0 collective-permute-done.10.refs_3_
  49.2 0.7 %shard_map.77 = bf16[1,1024,128]{2,1,0:T(8,128)(2,1)} custom-call(bf16[1,256,128]{2,1,0:T(8,128)(2,1)S(1)} %get-tuple-element.18.refs_0_, bf16[1,256,128]{2,1,0:T(8,128)(2,1)S(1)} %collective-permute-done.8.refs_1_, bf16[1,256,128]{2,1,0:T(8,128)(2,1)S(1)} %collective-permute-done.9.refs_2_, bf16[1,256,128]{2,1,0:T(8,128)(2,1)S(1)} %collective-permute-done.10.refs_3_, ...), custom_call_target="tpu_custom_call" | custom-call | bytes 524288 | tf_op jit(solution)/shard_map/pallas_call | solution.py:467
Async XLA Ops:
  0.6 10.6 %collective-permute-start.1 = (bf16[1,256,512]{2,1,0:T(8,128)(2,1)}, bf16[1,256,512]{2,1,0:T(8,128)(2,1)S(1)}, u32[]{:S(2)}, u32[]{:S(2)}) collective-permute-start(bf16[1,256,512]{2,1,0:T(8,128)(2,1)} %refs_4_.1), channel_id=1, source_target_pairs={{0,4},{4,12},{12,8},{8,0},{1,5},{5,13},{13,9},{9,1},{2,6},{6,14},{... | collective-permute-start | bytes 786440 | tf_op jit(solution)/shard_map/ppermute | solution.py:47
  3.7 10.0 %collective-permute-start = (bf16[1,256,512]{2,1,0:T(8,128)(2,1)}, bf16[1,256,512]{2,1,0:T(8,128)(2,1)S(1)}, u32[]{:S(2)}, u32[]{:S(2)}) collective-permute-start(bf16[1,256,512]{2,1,0:T(8,128)(2,1)} %refs_4_.1), channel_id=1, source_target_pairs={{0,2},{2,0},{1,3},{3,1},{4,6},{6,4},{5,7},{7,5},{8,10},{10,8},{9,1... | collective-permute-start | bytes 786440 | tf_op jit(solution)/shard_map/ppermute | solution.py:50
  11.2 8.4 %collective-permute-start.3 = (bf16[1,256,512]{2,1,0:T(8,128)(2,1)S(1)}, bf16[1,256,512]{2,1,0:T(8,128)(2,1)S(1)}, u32[]{:S(2)}, u32[]{:S(2)}) collective-permute-start(bf16[1,256,512]{2,1,0:T(8,128)(2,1)S(1)} %collective-permute-done.1.refs_1_.refs_5_), channel_id=1, source_target_pairs={{0,4},{4,12},{12,8},{8,0},{1,5},{5,13},{13,9},{9,1},{2,6},{6,14},{... | collective-permute-start | bytes 786440 | tf_op jit(solution)/shard_map/ppermute | solution.py:47
  12.2 14.2 %collective-permute-start.2 = (bf16[1,256,512]{2,1,0:T(8,128)(2,1)S(1)}, bf16[1,256,512]{2,1,0:T(8,128)(2,1)S(1)}, u32[]{:S(2)}, u32[]{:S(2)}) collective-permute-start(bf16[1,256,512]{2,1,0:T(8,128)(2,1)S(1)} %collective-permute-done.1.refs_1_.refs_5_), channel_id=1, source_target_pairs={{0,2},{2,0},{1,3},{3,1},{4,6},{6,4},{5,7},{7,5},{8,10},{10,8},{9,1... | collective-permute-start | bytes 786440 | tf_op jit(solution)/shard_map/ppermute | solution.py:50
  13.7 2.3 %copy-start = (bf16[3,3,256,1024]{3,2,1,0:T(8,128)(2,1)S(1)}, bf16[3,3,256,1024]{3,2,1,0:T(8,128)(2,1)}, u32[]{:S(2)}) copy-start(bf16[3,3,256,1024]{3,2,1,0:T(8,128)(2,1)} %weight.1) | copy-start | bytes 14155780
  16.0 0.7 %copy-start.2 = (f32[256]{0:T(256)S(1)}, f32[256]{0:T(256)}, u32[]{:S(2)}) copy-start(f32[256]{0:T(256)} %param.6) | copy-start | bytes 3076
  16.7 4.9 %copy-start.3 = (bf16[1,256,512]{2,1,0:T(8,128)(2,1)S(1)}, bf16[1,256,512]{2,1,0:T(8,128)(2,1)}, u32[]{:S(2)}) copy-start(bf16[1,256,512]{2,1,0:T(8,128)(2,1)} %refs_4_.1) | copy-start | bytes 786436
  19.6 10.2 %collective-permute-start.5 = (bf16[1,256,512]{2,1,0:T(8,128)(2,1)S(1)}, bf16[1,256,512]{2,1,0:T(8,128)(2,1)S(1)}, u32[]{:S(2)}, u32[]{:S(2)}) collective-permute-start(bf16[1,256,512]{2,1,0:T(8,128)(2,1)S(1)} %collective-permute-done.3.refs_1_.refs_2_.refs_6_), channel_id=1, source_target_pairs={{0,4},{4,12},{12,8},{8,0},{1,5},{5,13},{13,9},{9,1},{2,6},{6,14},{... | collective-permute-start | bytes 786440 | tf_op jit(solution)/shard_map/ppermute | solution.py:47
  20.4 7.7 %collective-permute-start.4 = (bf16[1,256,512]{2,1,0:T(8,128)(2,1)S(1)}, bf16[1,256,512]{2,1,0:T(8,128)(2,1)S(1)}, u32[]{:S(2)}, u32[]{:S(2)}) collective-permute-start(bf16[1,256,512]{2,1,0:T(8,128)(2,1)S(1)} %collective-permute-done.3.refs_1_.refs_2_.refs_6_), channel_id=1, source_target_pairs={{0,2},{2,0},{1,3},{3,1},{4,6},{6,4},{5,7},{7,5},{8,10},{10,8},{9,1... | collective-permute-start | bytes 786440 | tf_op jit(solution)/shard_map/ppermute | solution.py:50
  21.6 1.6 %copy-start.1 = (bf16[4,256,256]{2,1,0:T(8,128)(2,1)S(1)}, bf16[4,256,256]{2,1,0:T(8,128)(2,1)}, u32[]{:S(2)}) copy-start(bf16[4,256,256]{2,1,0:T(8,128)(2,1)} %cotangent.3) | copy-start | bytes 1572868
  23.4 9.3 %collective-permute-start.6 = (bf16[1,256,512]{2,1,0:T(8,128)(2,1)S(1)}, bf16[1,256,512]{2,1,0:T(8,128)(2,1)S(1)}, u32[]{:S(2)}, u32[]{:S(2)}) collective-permute-start(bf16[1,256,512]{2,1,0:T(8,128)(2,1)S(1)} %get-tuple-element.16), channel_id=1, source_target_pairs={{0,8},{4,0},{12,4},{8,12},{1,9},{5,1},{13,5},{9,13},{2,10},{6,2},{... | collective-permute-start | bytes 786440 | tf_op jit(solution)/shard_map/ppermute | solution.py:61
  25.6 7.5 %collective-permute-start.11 = (bf16[2,256,256]{2,1,0:T(8,128)(2,1)S(1)}, bf16[2,256,256]{2,1,0:T(8,128)(2,1)S(1)}, u32[]{:S(2)}, u32[]{:S(2)}) collective-permute-start(bf16[2,256,256]{2,1,0:T(8,128)(2,1)S(1)} %get-tuple-element.23), channel_id=1, source_target_pairs={{0,2},{2,0},{1,3},{3,1},{4,6},{6,4},{5,7},{7,5},{8,10},{10,8},{9,1... | collective-permute-start | bytes 786440 | tf_op jit(solution)/shard_map/ppermute | solution.py:62
  33.0 2.7 %collective-permute-start.7 = (f32[4,256,256]{2,1,0:T(8,128)S(1)}, f32[4,256,256]{2,1,0:T(8,128)S(1)}, u32[]{:S(2)}, u32[]{:S(2)}) collective-permute-start(f32[4,256,256]{2,1,0:T(8,128)S(1)} %shard_map.73.mine), channel_id=1, source_target_pairs={{0,1},{1,0},{2,3},{3,2},{4,5},{5,4},{6,7},{7,6},{8,9},{9,8},{10,11... | collective-permute-start | bytes 3145736 | tf_op jit(solution)/shard_map/ppermute | solution.py:498
  34.2 7.1 %collective-permute-start.12 = (f32[4,256,256]{2,1,0:T(8,128)S(1)}, f32[4,256,256]{2,1,0:T(8,128)S(1)}, u32[]{:S(2)}, u32[]{:S(2)}) collective-permute-start(f32[4,256,256]{2,1,0:T(8,128)S(1)} %shard_map.75.refs_0_), channel_id=1, source_target_pairs={{0,1},{1,0},{2,3},{3,2},{4,5},{5,4},{6,7},{7,6},{8,9},{9,8},{10,11... | collective-permute-start | bytes 3145736 | tf_op jit(solution)/shard_map/ppermute | solution.py:498
  34.8 6.6 %collective-permute-start.13 = (bf16[2,256,256]{2,1,0:T(8,128)(2,1)S(1)}, bf16[2,256,256]{2,1,0:T(8,128)(2,1)S(1)}, u32[]{:S(2)}, u32[]{:S(2)}) collective-permute-start(bf16[2,256,256]{2,1,0:T(8,128)(2,1)S(1)} %collective-permute-done.11.refs_0_.refs_2_), channel_id=1, source_target_pairs={{0,1},{1,0},{2,3},{3,2},{4,5},{5,4},{6,7},{7,6},{8,9},{9,8},{10,11... | collective-permute-start | bytes 786440 | tf_op jit(solution)/shard_map/ppermute | solution.py:506
  36.3 12.9 %collective-permute-start.8 = (bf16[1,256,128]{2,1,0:T(8,128)(2,1)S(1)}, bf16[1,256,128]{2,1,0:T(8,128)(2,1)S(1)}, u32[]{:S(2)}, u32[]{:S(2)}) collective-permute-start(bf16[1,256,128]{2,1,0:T(8,128)(2,1)S(1)} %get-tuple-element.19), channel_id=1, source_target_pairs={{0,4},{4,8},{8,12},{12,0},{1,5},{5,9},{9,13},{13,1},{2,6},{6,10},{... | collective-permute-start | bytes 196616 | tf_op jit(solution)/shard_map/ppermute | solution.py:503
  38.9 10.3 %collective-permute-start.9 = (bf16[1,256,128]{2,1,0:T(8,128)(2,1)S(1)}, bf16[1,256,128]{2,1,0:T(8,128)(2,1)S(1)}, u32[]{:S(2)}, u32[]{:S(2)}) collective-permute-start(bf16[1,256,128]{2,1,0:T(8,128)(2,1)S(1)} %get-tuple-element.20), channel_id=1, source_target_pairs={{0,8},{4,12},{8,0},{12,4},{1,9},{5,13},{9,1},{13,5},{2,10},{6,14},... | collective-permute-start | bytes 196616 | tf_op jit(solution)/shard_map/ppermute | solution.py:503
  41.0 8.2 %collective-permute-start.10 = (bf16[1,256,128]{2,1,0:T(8,128)(2,1)S(1)}, bf16[1,256,128]{2,1,0:T(8,128)(2,1)S(1)}, u32[]{:S(2)}, u32[]{:S(2)}) collective-permute-start(bf16[1,256,128]{2,1,0:T(8,128)(2,1)S(1)} %get-tuple-element.21), channel_id=1, source_target_pairs={{0,12},{4,0},{8,4},{12,8},{1,13},{5,1},{9,5},{13,9},{2,14},{6,2},{... | collective-permute-start | bytes 196616 | tf_op jit(solution)/shard_map/ppermute | solution.py:503
